TPU v7x, 32 devices: a whole 2x2x4 slice. The times are simulated.
32 devices in a mesh: groups: 2 (over y), expert: 8 (over z, core), beam: 2 (over x), head: 1.
Axes of the slice: x: 2, y: 2, z: 4, core: 2. Of those that a mesh axis runs over, the one named last changes fastest.
Arguments:
- states: bfloat16 [8, 4, 32, 128, 128], P('expert', ('groups', 'beam'), 'head'), parts along dimension 1, may hold values from -6 to 6
- qkv_rows: bfloat16 [3, 8, 4, 32, 128], P(None, 'expert', ('groups', 'beam'), 'head'), parts along dimension 2, may hold values from -6 to 6
- decay_rate: float32 [8, 4, 32], P('expert', ('groups', 'beam'), 'head'), parts along dimension 1, may hold values from 0.05 to 1
- parents: int32 [8, 4], P(None, ('groups', 'beam')), parts along dimension 1, may hold values from 0 to 7, as said below
- hidden: bfloat16 [8, 4, 3072], P('expert', ('groups', 'beam')), parts along dimension 1, may hold values from -6 to 6
- expert_ids: int32 [8, 4, 2], P('expert', 'groups'), parts along dimension 1, may hold values from 0 to 3, all different within a row; in each aligned block of 2 rows (0 to 1, 2 to 3, ..., all dimensions but the last counted through in order) at most 2 rows name the same one
- gate_weights: float32 [8, 4, 2], P('expert', 'groups'), parts along dimension 1, may hold values from 0.1 to 1
- w_gate: bfloat16 [8, 3072, 2304], P('expert', None, ('beam', 'head')), may hold values from -0.109375 to 0.109375
- w_up: bfloat16 [8, 3072, 2304], P('expert', None, ('beam', 'head')), may hold values from -0.109375 to 0.109375
- w_down: bfloat16 [8, 2304, 3072], P('expert', ('beam', 'head')), may hold values from -0.09375 to 0.09375
Outputs:
- new_states: bfloat16 [8, 4, 32, 128, 128], P('expert', ('groups', 'beam'), 'head'), parts along dimension 1
- readout: bfloat16 [8, 4, 32, 128], P('expert', ('groups', 'beam'), 'head'), parts along dimension 1
- mixed: bfloat16 [8, 4, 3072], P('expert', ('groups', 'beam'), 'head'), parts along dimension 1
There are 2 independent parts, one for each index of `groups`. A program takes and returns all parts, laid end to end along the dimension named above; an argument that names none is the same for every part. Nothing has to cross between parts.
Inputs may be any that keep to these rules, and one draw needn't show every extreme that they name: For every request, the 8 beams name exactly 4 distinct parents. `expert_ids`: each row names 2 different experts; among the 2 rows of one beam (aligned blocks of 2 rows) no expert is named by more than 2 rows.
All inputs are finite; a program needn't handle non-finite values.
Results may differ from a plain program's by a relative error of at most 0.0049.
Values may be sent and summed in bfloat16 or wider, within the bound.
A program may use at most 64 MiB of HBM per device.

v0:
```python
import jax
import jax.numpy as jnp
from jax import lax
from jax.sharding import PartitionSpec as P


def local(
    states, qkv_rows, decay_rate, parents, hidden, expert_ids, gate_weights, w_gate, w_up, w_down
):
    beam_index = lax.axis_index("expert")
    parent_ids = lax.dynamic_index_in_dim(parents, beam_index, 0, keepdims=False)
    shard_piece = lax.all_gather(states, "expert", axis=0, tiled=True)
    source_ids = jnp.arange(shard_piece.shape[0], dtype=jnp.int32)
    matches = source_ids[:, None] == parent_ids[None, :]
    chosen = jnp.sum(
        jnp.where(matches[:, :, None, None, None], shard_piece, jnp.zeros((), jnp.bfloat16)), axis=0
    )
    query = qkv_rows[0, 0].astype(jnp.float32)
    key_part = qkv_rows[1, 0].astype(jnp.float32)
    value_part = qkv_rows[2, 0].astype(jnp.float32)
    updated = (
        decay_rate[0][..., None, None] * chosen.astype(jnp.float32)
        + key_part[..., :, None] * value_part[..., None, :]
    )
    new_states = updated.astype(jnp.bfloat16)[None]
    raw_out = jnp.einsum("rhk,rhkv->rhv", query, updated, precision=lax.Precision.HIGHEST)
    readout = (
        raw_out * lax.rsqrt(jnp.mean(raw_out * raw_out, axis=-1, keepdims=True) + 1e-05)
    ).astype(jnp.bfloat16)[None]
    beam_block = lax.all_gather(hidden, "beam", axis=1, tiled=True)[0]
    route_ids = expert_ids[0]
    route_gates = gate_weights[0]
    request_count = beam_block.shape[0]
    top_count = route_ids.shape[1]
    expert_count = lax.axis_size("expert") // 2
    capacity = min(request_count, 2 * request_count * top_count // expert_count)
    expert_range = jnp.arange(expert_count, dtype=jnp.int32)
    flat_ids = route_ids.reshape(-1)
    one_hot = (flat_ids[None, :] == expert_range[:, None]).astype(jnp.int32)
    slot_rank = jnp.cumsum(one_hot, axis=1) - 1
    slot_range = jnp.arange(capacity, dtype=jnp.int32)
    assignment = one_hot[:, :, None] * (slot_rank[:, :, None] == slot_range[None, None, :]).astype(
        jnp.int32
    )
    placement = assignment.reshape(expert_count, request_count, top_count, capacity).sum(axis=2)
    gate_select = jnp.sum(
        jnp.where(
            route_ids[None, :, :] == expert_range[:, None, None],
            route_gates[None, :, :],
            jnp.zeros((), jnp.float32),
        ),
        axis=2,
    )
    combine_weight = placement.astype(jnp.float32) * gate_select[:, :, None]
    dispatched = jnp.einsum(
        "xrc,rd->xcd",
        placement.astype(jnp.bfloat16),
        beam_block,
        preferred_element_type=jnp.float32,
    ).astype(jnp.bfloat16)
    outgoing = jnp.repeat(dispatched, 2, axis=0)
    arrived = lax.all_to_all(outgoing, "expert", split_axis=0, concat_axis=0, tiled=True)
    gate_val = jnp.einsum("scd,df->scf", arrived, w_gate[0], preferred_element_type=jnp.float32)
    up_val = jnp.einsum("scd,df->scf", arrived, w_up[0], preferred_element_type=jnp.float32)
    middle = (jax.nn.silu(gate_val) * up_val).astype(jnp.bfloat16)
    partial_value = jnp.einsum("scf,fd->scd", middle, w_down[0], preferred_element_type=jnp.float32)
    returned = lax.all_to_all(partial_value, "expert", split_axis=0, concat_axis=0, tiled=True)
    paired = returned.reshape(expert_count, 2, capacity, returned.shape[2]).sum(axis=1)
    partial_rows = jnp.einsum(
        "xrc,xcd->rd", combine_weight, paired, precision=lax.Precision.HIGHEST
    )
    beam_size = lax.axis_size("beam")
    head_size = lax.axis_size("head")
    local_rows = request_count // beam_size
    model_width = partial_rows.shape[1]
    arranged = partial_rows.reshape(beam_size, local_rows, head_size, model_width // head_size)
    arranged = arranged.transpose(0, 2, 1, 3).reshape(
        beam_size * head_size * local_rows, model_width // head_size
    )
    summed = lax.psum_scatter(arranged, ("beam", "head"), scatter_dimension=0, tiled=True)
    mixed = summed.astype(jnp.bfloat16).reshape(1, local_rows, model_width // head_size)
    return (new_states, readout, mixed)


def solution(mesh):
    in_specs = (
        P("expert", ("groups", "beam"), "head", None, None),
        P(None, "expert", ("groups", "beam"), "head", None),
        P("expert", ("groups", "beam"), "head"),
        P(None, ("groups", "beam")),
        P("expert", ("groups", "beam"), None),
        P("expert", "groups", None),
        P("expert", "groups", None),
        P("expert", None, ("beam", "head")),
        P("expert", None, ("beam", "head")),
        P("expert", ("beam", "head"), None),
    )
    out_specs = (
        P("expert", ("groups", "beam"), "head", None, None),
        P("expert", ("groups", "beam"), "head", None),
        P("expert", ("groups", "beam"), "head"),
    )
    return jax.shard_map(local, mesh=mesh, in_specs=in_specs, out_specs=out_specs, check_vma=False)
```

profile of v0, /device:TPU:0, one launch (start us, length us, event | category | flops | bytes accessed | tf_op | source)
XLA Modules:
  0.0 116.9 jit_solution(6226458527341376144)
XLA Ops:
  7.2 0.7 all-gather.2.cloned.1.call-update
  7.9 0.8 eq.72
  8.8 0.7 fusion.39
  9.6 5.6 %all_gather.7 = bf16[1,2,3072]{2,0,1:T(2,128)(2,1)S(1)} all-gather(bf16[1,1,3072]{2,0,1:T(2,128)(2,1)} %bitcast.61), channel_id=1, replica_groups=mesh['groups'=2,'expert'=8,'beam'=2,'head'=1] {'beam'}, dimensions={1}, use_global_device_ids=true | all-gather | bytes 18432 | tf_op jit(solution)/shard_map/all_gather | solution.py:30
  15.4 0.7 broadcast_in_dim.51
  16.1 5.4 %all-to-all-start = ((bf16[8,2,3072]{2,1,0:T(2,128)(2,1)}), bf16[8,2,3072]{2,1,0:T(2,128)(2,1)S(1)}, u32[]{:S(2)}, u32[]{:S(2)}) async-start(bf16[8,2,3072]{2,1,0:T(2,128)(2,1)} %bitcast.16), calls=%async_computation | async-start | bytes 196608 | tf_op jit(solution)/shard_map/all_to_all | solution.py:62
  21.5 0.8 select_reduce_fusion.1
  22.3 8.8 %all-to-all-done = bf16[8,2,3072]{2,1,0:T(2,128)(2,1)S(1)} async-done(((bf16[8,2,3072]{2,1,0:T(2,128)(2,1)}), bf16[8,2,3072]{2,1,0:T(2,128)(2,1)S(1)}, u32[]{:S(2)}, u32[]{:S(2)}) %all-to-all-start) | async-done | bytes 98336 | tf_op jit(solution)/shard_map/all_to_all | solution.py:62
  31.1 4.0 %fusion.4 = f32[8,2,1152]{2,0,1:T(8,128)S(1)} fusion(bf16[1,3072,1152]{2,1,0:T(8,128)(2,1)} %param.17, bf16[8,2,3072]{2,1,0:T(2,128)(2,1)S(1)} %all-to-all-done), kind=kOutput, calls=%fused_computation.5 | convolution fusion | flops 113246208 | bytes 7249920 | tf_op jit(solution)/shard_map/scd,df->scf/dot_general | solution.py:63
  35.2 7.2 %fusion = f32[8,2,3072]{2,0,1:T(8,128)S(1)} fusion(bf16[1,1152,3072]{2,1,0:T(8,128)(2,1)} %param.19, bf16[1,3072,1152]{2,1,0:T(8,128)(2,1)} %param.18, bf16[8,2,3072]{2,1,0:T(2,128)(2,1)S(1)} %all-to-all-done, f32[8,2,1152]{2,0,1:T(8,128)S(1)} %fusion.4), kind=kOutput, calls=%fused_computation.1 | convolution fusion | flops 226603008 | bytes 14524416 | tf_op jit(solution)/shard_map/scf,fd->scd/dot_general | solution.py:66
  42.3 0.8 copy.37
  43.2 3.4 %all-to-all-start.1 = ((f32[8,2,3072]{2,1,0:T(2,128)}), f32[8,2,3072]{2,1,0:T(2,128)S(1)}, u32[]{:S(2)}, u32[]{:S(2)}) async-start(f32[8,2,3072]{2,1,0:T(2,128)} %copy.37), calls=%async_computation.1 | async-start | bytes 393216 | tf_op jit(solution)/shard_map/all_to_all | solution.py:67
  46.7 0.6 constant_dynamic-slice_fusion
  47.3 0.6 dynamic-slice
  47.8 0.7 iota_compare_fusion.2
  48.5 13.0 %all-to-all-done.1 = f32[8,2,3072]{2,1,0:T(2,128)S(1)} async-done(((f32[8,2,3072]{2,1,0:T(2,128)}), f32[8,2,3072]{2,1,0:T(2,128)S(1)}, u32[]{:S(2)}, u32[]{:S(2)}) %all-to-all-start.1) | async-done | bytes 196640 | tf_op jit(solution)/shard_map/all_to_all | solution.py:67
  61.6 0.4 convolution_bitcast_fusion
  62.0 8.3 %all-reduce = bf16[2,3072]{1,0:T(2,128)(2,1)S(1)} all-reduce(f32[2,3072]{1,0:T(2,128)S(1)} %convolution_bitcast_fusion), channel_id=2, replica_groups=mesh['groups'=2,'expert'=8,'beam'=2,'head'=1] {'beam','head'}, use_global_device_ids=true, to_apply=%region_6.7.clone | all-reduce | flops 6144 | bytes 36864
  70.3 1.2 %fusion.36 = bf16[1,1,3072]{2,1,0:T(2,128)(2,1)} fusion(bf16[2,3072]{1,0:T(2,128)(2,1)S(1)} %all-reduce, u32[]{:T(128)} %bitcast.27), kind=kLoop, calls=%fused_computation.37 | loop fusion | bytes 12292 | tf_op jit(solution)/shard_map/reshape | solution.py:81
  71.5 29.1 %all-gather.2.cloned.1.call-done = bf16[8,1,32,128,128]{4,3,2,1,0:T(8,128)(2,1)} async-done(((bf16[1,1,32,128,128]{4,3,2,1,0:T(8,128)(2,1)}), bf16[8,1,32,128,128]{4,3,2,1,0:T(8,128)(2,1)}) %all-gather.2.cloned.1.call-update) | async-done | bytes 8388624 | tf_op jit(solution)/shard_map/all_gather | solution.py:12
  100.6 5.4 %select_reduce_fusion = bf16[32,128,128]{2,1,0:T(8,128)(2,1)S(1)} fusion(bf16[8,1,32,128,128]{4,3,2,1,0:T(8,128)(2,1)} %all-gather.2.cloned.1.call-done, pred[8]{0:T(512)(128)(4,1)S(1)} %iota_compare_fusion.2), kind=kLoop, calls=%fused_computation | loop fusion | flops 7864320 | bytes 9437192 | tf_op jit(solution)/shard_map/reduce_sum | solution.py:15
  106.0 1.8 %fusion.14 = bf16[1,1,32,128,128]{4,3,2,1,0:T(8,128)(2,1)} fusion(bf16[32,128,128]{2,1,0:T(8,128)(2,1)S(1)} %select_reduce_fusion, f32[32,128]{1,0:T(8,128)S(1)} %get-tuple-element.5, f32[32,128]{1,0:T(8,128)S(1)} %get-tuple-element.4, f32[32]{0:T(128)S(1)} %bitcast.66), kind=kLoop, calls=%fused_computation.15 | loop fusion | flops 2621440 | bytes 2130048 | tf_op jit(solution)/shard_map/convert_element_type | solution.py:25
  107.9 1.4 %fusion.16 = f32[32,1,128]{2,1,0:T(1,128)S(1)} fusion(bf16[32,128,128]{2,1,0:T(8,128)(2,1)S(1)} %select_reduce_fusion, f32[32,128]{1,0:T(8,128)S(1)} %get-tuple-element.5, f32[32,128]{1,0:T(8,128)S(1)} %get-tuple-element.4, f32[32]{0:T(128)S(1)} %bitcast.67, bf16[32,128,1]{1,0,2:T(8,128)(2,1)S(1)} %get-tuple-element.3), kind=kOutput, calls=%fused_computation.17 | convolution fusion | flops 8388608 | bytes 1106048 | tf_op jit(solution)/shard_map/rhk,rhkv->rhv/dot_general | solution.py:26
  109.4 0.7 fusion.37
  (22 shorter events, 0.8 us)
Async XLA Ops:
  7.2 39.5 %copy-start = (s32[8,1]{0,1:T(1,128)S(1)}, s32[8,1]{0,1:T(1,128)}, u32[]{:S(2)}) copy-start(s32[8,1]{0,1:T(1,128)} %param.13) | copy-start | bytes 100
  7.2 93.4 %all-gather.2.cloned.1.call-start = ((), (), s32[]{:S(2)}) async-start(), calls=%async_computation.2 | async-start | bytes 9437184 | tf_op jit(solution)/shard_map/all_gather | solution.py:12
  16.1 15.0 %all-to-all-start = ((bf16[8,2,3072]{2,1,0:T(2,128)(2,1)}), bf16[8,2,3072]{2,1,0:T(2,128)(2,1)S(1)}, u32[]{:S(2)}, u32[]{:S(2)}) async-start(bf16[8,2,3072]{2,1,0:T(2,128)(2,1)} %bitcast.16), calls=%async_computation | async-start | bytes 196608 | tf_op jit(solution)/shard_map/all_to_all | solution.py:62
  35.1 12.1 %copy-start.3 = (u32[32]{0:T(128)S(1)}, u32[32]{0:T(128)}, u32[]{:S(2)}) copy-start(u32[32]{0:T(128)} %constant.45) | copy-start | bytes 388
  35.1 13.3 %copy-start.1 = (bf16[3,1,1,32,128]{4,3,2,1,0:T(8,128)(2,1)S(1)}, bf16[3,1,1,32,128]{4,3,2,1,0:T(8,128)(2,1)}, u32[]{:S(2)}) copy-start(bf16[3,1,1,32,128]{4,3,2,1,0:T(8,128)(2,1)} %param.11) | copy-start | bytes 73732
  42.3 63.7 %copy-start.2 = (f32[1,1,32]{2,1,0:T(1,128)S(1)}, f32[1,1,32]{2,1,0:T(1,128)}, u32[]{:S(2)}) copy-start(f32[1,1,32]{2,1,0:T(1,128)} %param.12) | copy-start | bytes 388
  43.2 18.3 %all-to-all-start.1 = ((f32[8,2,3072]{2,1,0:T(2,128)}), f32[8,2,3072]{2,1,0:T(2,128)S(1)}, u32[]{:S(2)}, u32[]{:S(2)}) async-start(f32[8,2,3072]{2,1,0:T(2,128)} %copy.37), calls=%async_computation.1 | async-start | bytes 393216 | tf_op jit(solution)/shard_map/all_to_all | solution.py:67
Sparse Core Ops, SparseCore 0:
  9.6 90.9 all-gather.1
where the time goes:
time: 117 us
  waiting for transfers between devices  51.6 us (44%)
  between operations  14.2 us (12%)
  blocking collectives  13.8 us (12%)
  matrix products  13.2 us (11%)
  other arithmetic  10.5 us (9%)
  starting transfers between devices  8.79 us (8%)
  local copies, waits for them, and re-layouts  4.78 us (4%)
    all_gather x1, waiting for transfers between devices, local(): shard_piece = lax.all_gather(states, 'expert', axis=0, tiled=True)  29.1 us
    all_to_all x1, waiting for transfers between devices, local(): lax.all_to_all(partial_value, 'expert', split_axis=0, concat_axis=0, tile...  13 us
    all_to_all x1, waiting for transfers between devices, local(): lax.all_to_all(outgoing, 'expert', split_axis=0, concat_axis=0, tiled=True)  8.83 us
    unnamed x1, blocking collectives  8.27 us
    dot_general x1, matrix products, local(): jnp.einsum('scf,fd->scd', middle, w_down[0], preferred_element_type=jnp.f...  7.16 us
    all_gather x1, blocking collectives, local(): beam_block = lax.all_gather(hidden, 'beam', axis=1, tiled=True)[0]  5.57 us
    reduce_sum x1, other arithmetic, local(): jnp.sum(jnp.where(matches[:, :, None, None, None], shard_piece, jnp.zeros...  5.44 us
    all_to_all x1, starting transfers between devices, local(): lax.all_to_all(outgoing, 'expert', split_axis=0, concat_axis=0, tiled=True)  5.37 us
  transfers between devices with their start and end apart: 3, of which 3 were waited for; matrix products, arithmetic and copies ran while one was open for 16% of the time, Pallas kernels for 0%

commit v1 on v0

--- a/solution.py
+++ b/solution.py
@@ -1,6 +1,8 @@
 import jax
 import jax.numpy as jnp
 from jax import lax
+from jax.experimental import pallas as pl
+from jax.experimental.pallas import tpu as pltpu
 from jax.sharding import PartitionSpec as P
 
 
@@ -82,6 +84,337 @@
     return (new_states, readout, mixed)
 
 
+CHUNKS = 8
+PIECES = 4
+SUB = 8
+
+
+def fused_kernel(
+    parents, decay, ids, gates, qkv, hid, states, w_gate, w_up, w_down,
+    new_states, readout, mixed,
+    row, rows, xb, gate_acc, up_acc, part, part_in, summed, final, raw,
+    wg, wu, wd, picked, fresh,
+    row_send, row_recv, block_send, block_recv, part_send, part_recv, sum_send, sum_recv,
+    w_sem, own_sem, out_sem, st_send, st_recv, fwd_send, pick_send,
+    *cand,
+):
+    e = lax.axis_index("expert")
+    be = lax.axis_index("beam")
+    z, c = e // 2, e % 2
+    q = c * 2 + be
+    side = z // 2
+    inner = (z == 1) | (z == 2)
+    outer = (z == 0) | (z == 3)
+    sib = z * 2 + (1 - c)
+    near = (1 + side) * 2 + c
+    far = (2 - side) * 2 + c
+    edge = 3 * side * 2 + c
+    far_edge = 3 * (1 - side) * 2 + c
+    chunks = len(cand)
+    heads = qkv.shape[3]
+    hc = heads // chunks
+    width = row.shape[1]
+    depth, hidden_units = w_gate.shape[1], w_gate.shape[2]
+    f32 = jnp.float32
+
+    def flip(index):
+        return index + 1 - 2 * c
+
+    def remote(src, dst, ssem, rsem, expert, beam):
+        return pltpu.make_async_remote_copy(
+            src_ref=src, dst_ref=dst, send_sem=ssem, recv_sem=rsem,
+            device_id={"expert": expert, "beam": beam}, device_id_type=pl.DeviceIdType.MESH,
+        )
+
+    barrier = pltpu.get_barrier_semaphore()
+    for step in range(1, 16):
+        other = (e * 2 + be + step) % 16
+        pl.semaphore_signal(
+            barrier, inc=1, device_id={"expert": other // 2, "beam": other % 2},
+            device_id_type=pl.DeviceIdType.MESH,
+        )
+
+    for p in range(PIECES):
+        span = pl.ds(p * (depth // PIECES), depth // PIECES)
+        pltpu.make_async_copy(w_gate.at[0, span], wg.at[span], w_sem.at[0, p]).start()
+        pltpu.make_async_copy(w_up.at[0, span], wu.at[span], w_sem.at[1, p]).start()
+    for p in range(PIECES):
+        span = pl.ds(p * (hidden_units // PIECES), hidden_units // PIECES)
+        pltpu.make_async_copy(w_down.at[0, span], wd.at[span], w_sem.at[2, p]).start()
+
+    def own(k):
+        return pltpu.make_async_copy(
+            states.at[0, 0, pl.ds(k * hc, hc)], cand[k].at[e], own_sem.at[k]
+        )
+
+    for k in range(chunks):
+        own(k).start()
+    for j in range(SUB):
+        row[j : j + 1, :] = hid[0, :, j * width : (j + 1) * width].astype(f32)
+    rows[q, z] = row[...]
+    pl.semaphore_wait(barrier, 15)
+
+    def row_copy(step):
+        there = (z + step) % 4
+        return remote(
+            row, rows.at[q, z], row_send.at[step - 1], row_recv.at[step - 1], there * 2 + c, be
+        )
+
+    def row_arrival(step):
+        come = (z - step + 4) % 4
+        return remote(
+            row, rows.at[q, come], row_send.at[step - 1], row_recv.at[step - 1], come * 2 + c, be
+        )
+
+    for step in range(1, 4):
+        row_copy(step).start()
+
+    def state_copy(k, slot, expert):
+        return remote(
+            states.at[0, 0, pl.ds(k * hc, hc)], cand[k].at[e],
+            st_send.at[k, slot], st_recv.at[k, e], expert, be,
+        )
+
+    def arrival(k, index):
+        return remote(
+            cand[k].at[index], cand[k].at[index], st_send.at[k, 0], st_recv.at[k, index], sib, be
+        )
+
+    def forward(k, slot, index):
+        return remote(
+            cand[k].at[index], cand[k].at[index],
+            fwd_send.at[k, slot], st_recv.at[k, index], sib, be,
+        )
+
+    def pick_copy(k):
+        return remote(
+            picked.at[k], cand[k].at[8], pick_send.at[k], st_recv.at[k, 8], edge, be
+        )
+
+    for k in range(chunks):
+        state_copy(k, 0, far).start()
+
+        @pl.when(outer)
+        def _():
+            state_copy(k, 1, near).start()
+
+        state_copy(k, 2, sib).start()
+
+    for step in range(1, 4):
+        row_arrival(step).wait_recv()
+
+    def block_copy(step):
+        to = (q + step) % 4
+        return remote(
+            rows.at[q], rows.at[q], block_send.at[step - 1], block_recv.at[step - 1],
+            z * 2 + to // 2, to % 2,
+        )
+
+    def block_arrival(step):
+        come = (q - step + 4) % 4
+        return remote(
+            rows.at[come], rows.at[come], block_send.at[step - 1], block_recv.at[step - 1],
+            z * 2 + come // 2, come % 2,
+        )
+
+    for step in range(1, 4):
+        block_copy(step).start()
+    for step in range(1, 4):
+        block_arrival(step).wait_recv()
+
+    for j in range(SUB):
+        xb[j] = rows[:, :, j, :].reshape(16, width).astype(jnp.bfloat16)
+    gate_acc[...] = jnp.zeros_like(gate_acc)
+    up_acc[...] = jnp.zeros_like(up_acc)
+    per = SUB // PIECES
+
+    @pl.loop(0, PIECES)
+    def _(p):
+        span = pl.ds(pl.multiple_of(p * (depth // PIECES), depth // PIECES), depth // PIECES)
+        pltpu.make_async_copy(w_gate.at[0, span], wg.at[span], w_sem.at[0, p]).wait()
+        pltpu.make_async_copy(w_up.at[0, span], wu.at[span], w_sem.at[1, p]).wait()
+        for i in range(per):
+            j = p * per + i
+            cut = pl.ds(pl.multiple_of(j * width, width), width)
+            gate_acc[...] += jnp.dot(xb[j], wg[cut, :], preferred_element_type=f32)
+            up_acc[...] += jnp.dot(xb[j], wu[cut, :], preferred_element_type=f32)
+
+    for p in range(PIECES):
+        span = pl.ds(p * (hidden_units // PIECES), hidden_units // PIECES)
+        pltpu.make_async_copy(w_down.at[0, span], wd.at[span], w_sem.at[2, p]).wait()
+    gate_val = gate_acc[...]
+    middle = (gate_val / (1.0 + jnp.exp(-gate_val)) * up_acc[...]).astype(jnp.bfloat16)
+    for j in range(SUB):
+        value = jnp.dot(
+            middle, wd[:, j * width : (j + 1) * width], preferred_element_type=f32
+        )
+        part[:, :, j, :] = value.reshape(4, 4, width)
+
+    def part_copy(step):
+        to = (q + step) % 4
+        return remote(
+            part.at[to], part_in.at[step - 1], part_send.at[step - 1], part_recv.at[step - 1],
+            z * 2 + to // 2, to % 2,
+        )
+
+    for step in range(1, 4):
+        part_copy(step).start()
+
+    flat = qkv[:, 0, 0].astype(f32).reshape(3 * heads, qkv.shape[4])
+    padded = jnp.concatenate([flat, jnp.zeros((128 - 3 * heads, 128), f32)], axis=0)
+    columns = padded.T
+    values = qkv[2, 0, 0].astype(f32)
+
+    def out_copy(k):
+        return pltpu.make_async_copy(
+            fresh.at[pl.ds(k * hc, hc)], new_states.at[0, 0, pl.ds(k * hc, hc)], out_sem.at[k]
+        )
+
+    def sum_copy(step):
+        there = (z + step) % 4
+        return remote(
+            summed.at[there], final.at[z], sum_send.at[step - 1], sum_recv.at[step - 1],
+            there * 2 + c, be,
+        )
+
+    def sum_arrival(step):
+        come = (z - step + 4) % 4
+        return remote(
+            summed.at[come], final.at[come], sum_send.at[step - 1], sum_recv.at[step - 1],
+            come * 2 + c, be,
+        )
+
+    mine = parents[e, 0]
+    wanted = parents[edge, 0]
+    index = jnp.where(inner | (mine // 2 == z), mine, 8)
+
+    for k in range(chunks):
+        own(k).wait()
+
+        @pl.when(inner)
+        def _():
+            for slot, source in enumerate((edge, far, far_edge)):
+                arrival(k, source).wait_recv()
+                forward(k, slot, source).start()
+            arrival(k, sib).wait_recv()
+            for source in (edge, far, far_edge):
+                arrival(k, flip(source)).wait_recv()
+            picked[k] = cand[k][wanted]
+            pick_copy(k).start()
+
+        @pl.when(outer)
+        def _():
+            arrival(k, sib).wait_recv()
+            arrival(k, 8).wait_recv()
+
+        for h in range(hc):
+            head = k * hc + h
+            parent = cand[k][index, h].astype(f32)
+            key = columns[:, heads + head : heads + head + 1]
+            query = columns[:, head : head + 1]
+            updated = decay[0, 0, head] * parent + key * values[head : head + 1, :]
+            fresh[head] = updated.astype(jnp.bfloat16)
+            raw[head : head + 1, :] = jnp.sum(query * updated, axis=0, keepdims=True)
+        out_copy(k).start()
+
+        if k == 0:
+            for step in range(1, 4):
+                part_copy(step).wait_recv()
+            summed[...] = part[q] + part_in[0] + part_in[1] + part_in[2]
+            for step in range(1, 4):
+                sum_copy(step).start()
+            final[z] = summed[z]
+
+    raw_out = raw[...]
+    scale = lax.rsqrt(jnp.mean(raw_out * raw_out, axis=-1, keepdims=True) + 1e-05)
+    readout[0, 0] = (raw_out * scale).astype(jnp.bfloat16)
+
+    for step in range(1, 4):
+        sum_arrival(step).wait_recv()
+    total = jnp.zeros((SUB, width), f32)
+    for x in range(4):
+        weight = jnp.float32(0.0)
+        for t in range(ids.shape[2]):
+            weight += jnp.where(ids[0, be, t] == x, gates[0, be, t], jnp.float32(0.0))
+        total += weight * final[x]
+    for j in range(SUB):
+        mixed[0, :, j * width : (j + 1) * width] = total[j : j + 1, :].astype(jnp.bfloat16)
+
+    for step in range(1, 4):
+        row_copy(step).wait_send()
+        block_copy(step).wait_send()
+        part_copy(step).wait_send()
+        sum_copy(step).wait_send()
+    for k in range(chunks):
+        out_copy(k).wait()
+        state_copy(k, 0, far).wait_send()
+        state_copy(k, 2, sib).wait_send()
+
+        @pl.when(outer)
+        def _():
+            state_copy(k, 1, near).wait_send()
+
+        @pl.when(inner)
+        def _():
+            for slot, source in enumerate((edge, far, far_edge)):
+                forward(k, slot, source).wait_send()
+            pick_copy(k).wait_send()
+
+
+def fused(
+    states, qkv_rows, decay_rate, parents, hidden, expert_ids, gate_weights, w_gate, w_up, w_down
+):
+    heads, dim = states.shape[2], states.shape[3]
+    depth, units = w_gate.shape[1], w_gate.shape[2]
+    width = depth // SUB
+    hc = heads // CHUNKS
+    f32, bf16 = jnp.float32, jnp.bfloat16
+    smem = pl.BlockSpec(memory_space=pltpu.SMEM)
+    vmem = pl.BlockSpec(memory_space=pltpu.VMEM)
+    anywhere = pl.BlockSpec(memory_space=pl.ANY)
+    dma = pltpu.SemaphoreType.DMA
+    scratch = [
+        pltpu.VMEM((SUB, width), f32),
+        pltpu.VMEM((4, 4, SUB, width), f32),
+        pltpu.VMEM((SUB, 16, width), bf16),
+        pltpu.VMEM((16, units), f32),
+        pltpu.VMEM((16, units), f32),
+        pltpu.VMEM((4, 4, SUB, width), f32),
+        pltpu.VMEM((3, 4, SUB, width), f32),
+        pltpu.VMEM((4, SUB, width), f32),
+        pltpu.VMEM((4, SUB, width), f32),
+        pltpu.VMEM((heads, dim), f32),
+        pltpu.VMEM((depth, units), bf16),
+        pltpu.VMEM((depth, units), bf16),
+        pltpu.VMEM((units, depth), bf16),
+        pltpu.VMEM((CHUNKS, hc, dim, dim), bf16),
+        pltpu.VMEM((heads, dim, dim), bf16),
+        dma((3,)), dma((3,)), dma((3,)), dma((3,)), dma((3,)), dma((3,)), dma((3,)), dma((3,)),
+        dma((3, PIECES)), dma((CHUNKS,)), dma((CHUNKS,)),
+        dma((CHUNKS, 3)), dma((CHUNKS, 9)), dma((CHUNKS, 3)), dma((CHUNKS,)),
+    ] + [pltpu.VMEM((9, hc, dim, dim), bf16) for _ in range(CHUNKS)]
+    return pl.pallas_call(
+        fused_kernel,
+        out_shape=(
+            jax.ShapeDtypeStruct(states.shape, bf16),
+            jax.ShapeDtypeStruct(qkv_rows.shape[1:], bf16),
+            jax.ShapeDtypeStruct(hidden.shape, bf16),
+        ),
+        in_specs=[smem] * 4 + [vmem] * 2 + [anywhere] * 4,
+        out_specs=(anywhere, vmem, vmem),
+        scratch_shapes=scratch,
+        compiler_params=pltpu.CompilerParams(
+            collective_id=0, has_side_effects=True, vmem_limit_bytes=50 * 1024 * 1024
+        ),
+        cost_estimate=pl.CostEstimate(
+            flops=6 * 16 * depth * units, bytes_accessed=6 * depth * units, transcendentals=0
+        ),
+    )(
+        parents, decay_rate, expert_ids, gate_weights, qkv_rows, hidden, states,
+        w_gate, w_up, w_down,
+    )
+
+
 def solution(mesh):
     in_specs = (
         P("expert", ("groups", "beam"), "head", None, None),
@@ -100,4 +433,7 @@
         P("expert", ("groups", "beam"), "head", None),
         P("expert", ("groups", "beam"), "head"),
     )
-    return jax.shard_map(local, mesh=mesh, in_specs=in_specs, out_specs=out_specs, check_vma=False)
+    sizes = mesh.shape
+    fits = sizes["expert"] == 8 and sizes["beam"] == 2 and sizes["head"] == 1
+    body = fused if fits else local
+    return jax.shard_map(body, mesh=mesh, in_specs=in_specs, out_specs=out_specs, check_vma=False)

time: 117 us -> 71.3 us (0.61)
  Pallas kernels: 0 us -> 62.7 us
  waiting for transfers between devices: 51.6 us -> 0 us
  blocking collectives: 13.8 us -> 0 us
  between operations: 14.2 us -> 0.65 us
  matrix products: 13.2 us -> 0 us
  other arithmetic: 10.5 us -> 0 us
  starting transfers between devices: 8.79 us -> 0 us
  local copies, waits for them, and re-layouts: 4.78 us -> 7.58 us
    pallas_call x0 -> x1, Pallas kernels: none -> 62.7 us  [fused(): pl.pallas_call(fused_kernel, out_shape=(jax.ShapeDtypeStruct(states.shape...]
    all_gather x1 -> x0, waiting for transfers between devices: 29.1 us -> none  [local(): shard_piece = lax.all_gather(states, 'expert', axis=0, tiled=True)]
    all_to_all x2 -> x0, waiting for transfers between devices: 21.8 us -> none  [the longest x1 13 us: local(): lax.all_to_all(partial_value, 'expert', split_axis=0, concat_axis=0, tile...]
    dot_general x5 -> x0, matrix products: 13.2 us -> none  [the longest x1 7.16 us: local(): jnp.einsum('scf,fd->scd', middle, w_down[0], preferred_element_type=jnp.f...]
    all_to_all x2 -> x0, starting transfers between devices: 8.76 us -> none  [the longest x1 5.37 us: local(): lax.all_to_all(outgoing, 'expert', split_axis=0, concat_axis=0, tiled=True)]
    unnamed x1 -> x0, blocking collectives: 8.27 us -> none
    unnamed x9 -> x16, local copies, waits for them, and re-layouts: 0.58 us -> 7.58 us
    reduce_sum x5 -> x0, other arithmetic: 6.44 us -> none  [the longest x1 5.44 us: local(): jnp.sum(jnp.where(matches[:, :, None, None, None], shard_piece, jnp.zeros...]
  transfers between devices with their start and end apart: 3 -> 0, of which waited for: 3 -> 0; matrix products, arithmetic and copies ran while one was open for 16% -> 0% of each run, Pallas kernels for 0% -> 0%
where the time goes in v1:
time: 71.3 us; the launch traced here: 71 us
  Pallas kernels  62.7 us (88%)
  local copies, waits for them, and re-layouts  7.58 us (11%)
    pallas_call x1, Pallas kernels, fused(): pl.pallas_call(fused_kernel, out_shape=(jax.ShapeDtypeStruct(states.shape...  62.7 us
    unnamed x16, local copies, waits for them, and re-layouts  7.58 us

profile of v1, /device:TPU:0, one launch (start us, length us, event | category | flops | bytes accessed | tf_op | source)
XLA Modules:
  0.0 71.0 jit_solution(14526744199125459916)
XLA Ops:
  0.6 0.7 %copy.13.parents = s32[8,1]{1,0:T(8,128)S(1)} copy(s32[8,1]{0,1:T(1,128)} %param.13) | data formatting | bytes 64 | tf_op args[3]
  1.4 0.0 copy-start
  1.4 1.2 %copy-done = bf16[1,1,32,128,128]{4,3,2,1,0:T(8,128)(2,1)S(1)} copy-done((bf16[1,1,32,128,128]{4,3,2,1,0:T(8,128)(2,1)S(1)}, bf16[1,1,32,128,128]{4,3,2,1,0:T(8,128)(2,1)}, u32[]{:S(2)}) %copy-start) | copy-done | bytes 1048600
  2.6 0.0 copy-start.1
  2.6 0.7 %copy-done.1 = bf16[3,1,1,32,128]{4,3,2,1,0:T(8,128)(2,1)S(1)} copy-done((bf16[3,1,1,32,128]{4,3,2,1,0:T(8,128)(2,1)S(1)}, bf16[3,1,1,32,128]{4,3,2,1,0:T(8,128)(2,1)}, u32[]{:S(2)}) %copy-start.1) | copy-done | bytes 24600
  3.3 0.0 copy-start.2
  3.3 0.7 copy-done.2
  4.0 0.0 copy-start.3
  4.0 0.7 copy-done.3
  4.7 0.0 copy-start.4
  4.7 0.7 copy-done.4
  5.4 0.0 copy-start.5
  5.4 0.7 copy-done.5
  6.0 62.7 %shard_map.121 = (bf16[1,1,32,128,128]{4,3,2,1,0:T(8,128)(2,1)S(1)}, bf16[1,1,32,128]{3,2,1,0:T(8,128)(2,1)S(1)}, bf16[1,1,3072]{2,1,0:T(2,128)(2,1)S(1)}) custom-call(s32[8,1]{1,0:T(8,128)S(1)} %copy.13.parents, f32[1,1,32]{2,1,0:T(1,128)S(1)} %copy-done.5, s32[1,2,2]{2,1,0:T(2,128)S(1)} %copy-done.3, f32[1,2,2]{2,1,0:T(2,128)S(1)} %copy-done.4, ...), custom_call_target="tpu_custom_call" | custom-call | flops 339738624 | bytes 21233664 | tf_op jit(solution)/shard_map/pallas_call | solution.py:396
  68.8 1.0 %copy.17 = bf16[1,1,32,128,128]{4,3,2,1,0:T(8,128)(2,1)} copy(bf16[1,1,32,128,128]{4,3,2,1,0:T(8,128)(2,1)S(1)} %get-tuple-element.6) | data formatting | bytes 2097152
  69.8 0.6 copy.18
  70.4 0.6 copy.19
Async XLA Ops:
  1.4 1.2 %copy-start = (bf16[1,1,32,128,128]{4,3,2,1,0:T(8,128)(2,1)S(1)}, bf16[1,1,32,128,128]{4,3,2,1,0:T(8,128)(2,1)}, u32[]{:S(2)}) copy-start(bf16[1,1,32,128,128]{4,3,2,1,0:T(8,128)(2,1)} %states.1) | copy-start | bytes 3145732
  2.6 0.7 %copy-start.1 = (bf16[3,1,1,32,128]{4,3,2,1,0:T(8,128)(2,1)S(1)}, bf16[3,1,1,32,128]{4,3,2,1,0:T(8,128)(2,1)}, u32[]{:S(2)}) copy-start(bf16[3,1,1,32,128]{4,3,2,1,0:T(8,128)(2,1)} %qkv.1) | copy-start | bytes 73732
  3.3 0.7 copy-start.2
  4.0 0.7 copy-start.3
  4.7 0.7 copy-start.4
  5.4 0.7 copy-start.5

commit v2 on v1

--- a/solution.py
+++ b/solution.py
@@ -1,3 +1,4 @@
+import functools
 import jax
 import jax.numpy as jnp
 from jax import lax
@@ -415,6 +416,519 @@
     )
 
 
+SLOTS = 3
+STEPS = 16
+
+
+def routed_kernel(
+    parents_in, decay_in, ids_in, gates_in, qkv_in, hid_in, states, w_gate, w_up, w_down,
+    new_states, readout, mixed, flag,
+    row, rows, xb, gate_acc, up_acc, middle, part, part_in, summed, final, raw,
+    wg, wu, wd, picked, extra, edged, fresh, mark, marks,
+    parents, decay, ids, gates, qkv, hid,
+    small_sem, mark_send, mark_recv,
+    row_send, row_recv, block_send, block_recv, part_send, part_recv, sum_send, sum_recv,
+    w_sem, own_sem, out_sem, st_send, a_recv, b_recv, fwd_send, pick_send,
+    *cand,
+):
+    steps = len(cand) // 2
+    near_set, far_set = cand[:steps], cand[steps:]
+    g = lax.axis_index("groups")
+    e = lax.axis_index("expert")
+    be = lax.axis_index("beam")
+    z, c = e // 2, e % 2
+    q = c * 2 + be
+    side = z // 2
+    inner = (z == 1) | (z == 2)
+    outer = (z == 0) | (z == 3)
+    sib = z * 2 + (1 - c)
+    near = (1 + side) * 2 + c
+    far = (2 - side) * 2 + c
+    edge = 3 * side * 2 + c
+    heads = qkv.shape[3]
+    hc = heads // steps
+    width = row.shape[1]
+    depth, hidden_units = w_gate.shape[1], w_gate.shape[2]
+    f32 = jnp.float32
+
+    def remote(src, dst, ssem, rsem, expert, beam):
+        return pltpu.make_async_remote_copy(
+            src_ref=src, dst_ref=dst, send_sem=ssem, recv_sem=rsem,
+            device_id={"expert": expert, "beam": beam}, device_id_type=pl.DeviceIdType.MESH,
+        )
+
+    small = [
+        pltpu.make_async_copy(src, dst, small_sem.at[i])
+        for i, (src, dst) in enumerate(
+            (
+                (hid_in, hid), (parents_in, parents), (qkv_in, qkv),
+                (decay_in, decay), (ids_in, ids), (gates_in, gates),
+            )
+        )
+    ]
+    for copy in small:
+        copy.start()
+
+    barrier = pltpu.get_barrier_semaphore()
+    for step in range(1, 16):
+        other = (e * 2 + be + step) % 16
+        pl.semaphore_signal(
+            barrier, inc=1, device_id={"expert": other // 2, "beam": other % 2},
+            device_id_type=pl.DeviceIdType.MESH,
+        )
+    for beam in range(2):
+        pl.semaphore_signal(
+            barrier, inc=1, device_id={"groups": 1 - g, "beam": beam},
+            device_id_type=pl.DeviceIdType.MESH,
+        )
+
+    def own(k):
+        return pltpu.make_async_copy(
+            states.at[0, 0, pl.ds(k * hc, hc)], near_set[k].at[c], own_sem.at[k]
+        )
+
+    small[0].wait()
+    for j in range(SUB):
+        row[j : j + 1, :] = hid[0, :, j * width : (j + 1) * width].astype(f32)
+    rows[q, z] = row[...]
+
+    small[1].wait()
+    zero, one = jnp.int32(0), jnp.int32(1)
+
+    def needed(base, takers):
+        found = []
+        for j in range(4):
+            hit = zero
+            for i in range(4):
+                hit = jnp.where(parents[0, takers + i] == base + j, one, hit)
+            found.append(hit)
+        return found
+
+    my_base, other_base = 4 * side, 4 * (1 - side)
+    going = needed(my_base, other_base)
+    coming = needed(other_base, my_base)
+
+    def rank_of(found, j):
+        total = zero
+        for i in range(4):
+            total += jnp.where(i < j, found[i], zero)
+        return jnp.minimum(total, SLOTS - 1)
+
+    def entry_of(j):
+        return (j & 1) + jnp.where(((j >> 1) & 1) == 1 - side, 0, 2)
+
+    def chosen(slot):
+        pick, before = zero, zero
+        for j in range(4):
+            pick = jnp.where((going[j] == 1) & (before == slot), jnp.int32(j), pick)
+            before += going[j]
+        return entry_of(pick)
+
+    slot_entry = [chosen(slot) for slot in range(SLOTS)]
+    my_slot = jnp.where(c == 0, slot_entry[0], slot_entry[1])
+    overflow = (sum(going) > SLOTS) | (sum(coming) > SLOTS)
+    mark[...] = jnp.zeros_like(mark) + jnp.where(overflow, f32(1.0), f32(0.0))
+
+    wanted = parents[0, edge]
+    edge_far = (wanted >> 2) != side
+    edge_near_entry = entry_of(wanted & 3)
+    edge_slot = rank_of(coming, wanted & 3)
+    mine = parents[0, e]
+    chip_own = (mine >> 1) == z
+    use_far = jnp.where(inner, jnp.where((mine >> 2) != side, one, zero), jnp.where(chip_own, zero, one)) == 1
+    near_entry = jnp.where(inner, entry_of(mine & 3), mine & 1)
+    far_entry = jnp.where(inner, rank_of(coming, mine & 3), zero)
+
+    pl.semaphore_wait(barrier, 17)
+
+    def row_copy(step):
+        there = (z + step) % 4
+        return remote(
+            row, rows.at[q, z], row_send.at[step - 1], row_recv.at[step - 1], there * 2 + c, be
+        )
+
+    def row_arrival(step):
+        come = (z - step + 4) % 4
+        return remote(
+            row, rows.at[q, come], row_send.at[step - 1], row_recv.at[step - 1], come * 2 + c, be
+        )
+
+    def state_copy(k, slot, expert, entry):
+        return remote(
+            states.at[0, 0, pl.ds(k * hc, hc)], near_set[k].at[entry],
+            st_send.at[k, slot], a_recv.at[k, entry], expert, be,
+        )
+
+    def near_arrival(k, entry):
+        there = near_set[k].at[entry]
+        return remote(there, there, st_send.at[k, 0], a_recv.at[k, entry], sib, be)
+
+    def far_arrival(k, entry):
+        there = far_set[k].at[entry]
+        return remote(there, there, st_send.at[k, 0], b_recv.at[k, entry], sib, be)
+
+    def near_forward(k):
+        there = near_set[k].at[2 + c]
+        return remote(there, there, fwd_send.at[k, 0], a_recv.at[k, 2 + c], sib, be)
+
+    def far_forward(k, slot, entry):
+        there = far_set[k].at[entry]
+        return remote(there, there, fwd_send.at[k, slot], b_recv.at[k, entry], sib, be)
+
+    def slot_copy(k):
+        return remote(
+            picked.at[k], far_set[k].at[c], pick_send.at[k, 0], b_recv.at[k, c], far, be
+        )
+
+    def extra_copy(k):
+        return remote(
+            extra.at[k // 2], far_set[k].at[2], pick_send.at[k, 1], b_recv.at[k, 2], far, be
+        )
+
+    def edge_copy(k):
+        return remote(
+            edged.at[k], far_set[k].at[0], pick_send.at[k, 2], b_recv.at[k, 0], edge, be
+        )
+
+    for k in range(steps):
+        @pl.when(outer)
+        def _():
+            state_copy(k, 1, near, 2 + c).start()
+
+        state_copy(k, 0, sib, c).start()
+        own(k).start()
+        if k == 0:
+            for step in range(1, 4):
+                row_copy(step).start()
+
+    def mark_copy(step):
+        column = (g * 2 + be + step) % 4
+        return pltpu.make_async_remote_copy(
+            src_ref=mark, dst_ref=marks.at[step - 1], send_sem=mark_send.at[step - 1],
+            recv_sem=mark_recv.at[step - 1],
+            device_id={"groups": column // 2, "beam": column % 2},
+            device_id_type=pl.DeviceIdType.MESH,
+        )
+
+    for step in range(1, 4):
+        mark_copy(step).start()
+
+    for p in range(PIECES):
+        span = pl.ds(p * (depth // PIECES), depth // PIECES)
+        pltpu.make_async_copy(w_gate.at[0, span], wg.at[span], w_sem.at[0, p]).start()
+        pltpu.make_async_copy(w_up.at[0, span], wu.at[span], w_sem.at[1, p]).start()
+    for p in range(PIECES):
+        span = pl.ds(p * (hidden_units // PIECES), hidden_units // PIECES)
+        pltpu.make_async_copy(w_down.at[0, span], wd.at[span], w_sem.at[2, p]).start()
+
+    def pass_near(k):
+        @pl.when(inner)
+        def _():
+            near_arrival(k, 2 + c).wait_recv()
+            near_forward(k).start()
+
+    def send_slots(k):
+        own(k).wait()
+        near_arrival(k, 1 - c).wait_recv()
+
+        @pl.when(inner)
+        def _():
+            near_arrival(k, 3 - c).wait_recv()
+            picked[k] = near_set[k][my_slot]
+            slot_copy(k).start()
+
+        @pl.when(inner & (c == k % 2))
+        def _():
+            extra[k // 2] = near_set[k][slot_entry[2]]
+            extra_copy(k).start()
+
+    def pass_far(k):
+        @pl.when(inner)
+        def _():
+            far_arrival(k, c).wait_recv()
+            far_forward(k, 1, c).start()
+
+        @pl.when(inner & (c == k % 2))
+        def _():
+            far_arrival(k, 2).wait_recv()
+            far_forward(k, 2, 2).start()
+
+    def out_copy(k):
+        return pltpu.make_async_copy(
+            fresh.at[pl.ds(k * hc, hc)], new_states.at[0, 0, pl.ds(k * hc, hc)], out_sem.at[k]
+        )
+
+    def send_edge(k):
+        @pl.when(inner)
+        def _():
+            far_arrival(k, 1 - c).wait_recv()
+
+        @pl.when(inner & (c != k % 2))
+        def _():
+            far_arrival(k, 2).wait_recv()
+
+        @pl.when(inner)
+        def _():
+            edged[k] = jnp.where(edge_far, far_set[k][edge_slot], near_set[k][edge_near_entry])
+            edge_copy(k).start()
+
+    def finish(k):
+        @pl.when(outer)
+        def _():
+            far_arrival(k, 0).wait_recv()
+
+        for h in range(hc):
+            head = k * hc + h
+            parent = jnp.where(
+                use_far, far_set[k][far_entry, h], near_set[k][near_entry, h]
+            ).astype(f32)
+            key = columns[:, heads + head : heads + head + 1]
+            query = columns[:, head : head + 1]
+            updated = decay[0, 0, head] * parent + key * values[head : head + 1, :]
+            fresh[head] = updated.astype(jnp.bfloat16)
+            raw[head : head + 1, :] = jnp.sum(query * updated, axis=0, keepdims=True)
+        out_copy(k).start()
+
+    def block_copy(step):
+        to = (q + step) % 4
+        return remote(
+            rows.at[q], rows.at[q], block_send.at[step - 1], block_recv.at[step - 1],
+            z * 2 + to // 2, to % 2,
+        )
+
+    def block_arrival(step):
+        come = (q - step + 4) % 4
+        return remote(
+            rows.at[come], rows.at[come], block_send.at[step - 1], block_recv.at[step - 1],
+            z * 2 + come // 2, come % 2,
+        )
+
+    def gather_first():
+        for step in range(1, 4):
+            row_arrival(step).wait_recv()
+        for step in range(1, 4):
+            block_copy(step).start()
+
+    def gather_second():
+        for step in range(1, 4):
+            block_arrival(step).wait_recv()
+        for j in range(SUB):
+            xb[j] = rows[:, :, j, :].reshape(16, width).astype(jnp.bfloat16)
+        gate_acc[...] = jnp.zeros_like(gate_acc)
+        up_acc[...] = jnp.zeros_like(up_acc)
+
+    per = SUB // PIECES
+
+    def first_dots(p):
+        span = pl.ds(p * (depth // PIECES), depth // PIECES)
+        pltpu.make_async_copy(w_gate.at[0, span], wg.at[span], w_sem.at[0, p]).wait()
+        pltpu.make_async_copy(w_up.at[0, span], wu.at[span], w_sem.at[1, p]).wait()
+        for i in range(per):
+            j = p * per + i
+            cut = pl.ds(j * width, width)
+            gate_acc[...] += jnp.dot(xb[j], wg[cut, :], preferred_element_type=f32)
+            up_acc[...] += jnp.dot(xb[j], wu[cut, :], preferred_element_type=f32)
+
+    def activate():
+        for p in range(PIECES):
+            span = pl.ds(p * (hidden_units // PIECES), hidden_units // PIECES)
+            pltpu.make_async_copy(w_down.at[0, span], wd.at[span], w_sem.at[2, p]).wait()
+        gate_val = gate_acc[...]
+        middle[...] = (gate_val / (1.0 + jnp.exp(-gate_val)) * up_acc[...]).astype(jnp.bfloat16)
+
+    def second_dots(p):
+        for i in range(per):
+            j = p * per + i
+            value = jnp.dot(
+                middle[...], wd[:, j * width : (j + 1) * width], preferred_element_type=f32
+            )
+            part[:, :, j, :] = value.reshape(4, 4, width)
+
+    def part_copy(step):
+        to = (q + step) % 4
+        return remote(
+            part.at[to], part_in.at[step - 1], part_send.at[step - 1], part_recv.at[step - 1],
+            z * 2 + to // 2, to % 2,
+        )
+
+    def sum_copy(step):
+        there = (z + step) % 4
+        return remote(
+            summed.at[there], final.at[z], sum_send.at[step - 1], sum_recv.at[step - 1],
+            there * 2 + c, be,
+        )
+
+    def sum_arrival(step):
+        come = (z - step + 4) % 4
+        return remote(
+            summed.at[come], final.at[come], sum_send.at[step - 1], sum_recv.at[step - 1],
+            come * 2 + c, be,
+        )
+
+    def send_parts():
+        for step in range(1, 4):
+            part_copy(step).start()
+
+    def send_sums():
+        for step in range(1, 4):
+            part_copy(step).wait_recv()
+        summed[...] = part[q] + part_in[0] + part_in[1] + part_in[2]
+        for step in range(1, 4):
+            sum_copy(step).start()
+        final[z] = summed[z]
+
+    pass_near(0)
+    for copy in small[2:]:
+        copy.wait()
+    flat = qkv[:, 0, 0].astype(f32).reshape(3 * heads, qkv.shape[4])
+    padded = jnp.concatenate([flat, jnp.zeros((128 - 3 * heads, 128), f32)], axis=0)
+    columns = padded.T
+    values = qkv[2, 0, 0].astype(f32)
+
+    work = [gather_first, gather_second]
+    work += [functools.partial(first_dots, p) for p in range(PIECES)]
+    work += [activate]
+    work += [functools.partial(second_dots, p) for p in range(PIECES)]
+    work += [send_parts]
+    share = -(-len(work) // steps)
+    lag, last = 3, 4
+    for i in range(steps + last):
+        if i < steps:
+            send_slots(i)
+        if i + 1 < steps:
+            pass_near(i + 1)
+        if 0 <= i - lag < steps:
+            pass_far(i - lag)
+        for unit in work[i * share : (i + 1) * share]:
+            unit()
+        if 0 <= i - last < steps:
+            send_edge(i - last)
+            finish(i - last)
+        if i == steps:
+            send_sums()
+
+    raw_out = raw[...]
+    scale = lax.rsqrt(jnp.mean(raw_out * raw_out, axis=-1, keepdims=True) + 1e-05)
+    readout[0, 0] = (raw_out * scale).astype(jnp.bfloat16)
+
+    for step in range(1, 4):
+        sum_arrival(step).wait_recv()
+    total = jnp.zeros((SUB, width), f32)
+    for x in range(4):
+        weight = jnp.float32(0.0)
+        for t in range(ids.shape[2]):
+            weight += jnp.where(ids[0, be, t] == x, gates[0, be, t], jnp.float32(0.0))
+        total += weight * final[x]
+    for j in range(SUB):
+        mixed[0, :, j * width : (j + 1) * width] = total[j : j + 1, :].astype(jnp.bfloat16)
+
+    for step in range(1, 4):
+        mark_copy(step).wait_recv()
+    flag[...] = mark[...] + marks[0] + marks[1] + marks[2]
+
+    for step in range(1, 4):
+        mark_copy(step).wait_send()
+        row_copy(step).wait_send()
+        block_copy(step).wait_send()
+        part_copy(step).wait_send()
+        sum_copy(step).wait_send()
+    for k in range(steps):
+        out_copy(k).wait()
+        state_copy(k, 0, sib, c).wait_send()
+
+        @pl.when(outer)
+        def _():
+            state_copy(k, 1, near, 2 + c).wait_send()
+
+        @pl.when(inner)
+        def _():
+            near_forward(k).wait_send()
+            slot_copy(k).wait_send()
+            far_forward(k, 1, c).wait_send()
+            edge_copy(k).wait_send()
+
+        @pl.when(inner & (c == k % 2))
+        def _():
+            extra_copy(k).wait_send()
+            far_forward(k, 2, 2).wait_send()
+
+
+def routed(
+    states, qkv_rows, decay_rate, parents, hidden, expert_ids, gate_weights, w_gate, w_up, w_down
+):
+    heads, dim = states.shape[2], states.shape[3]
+    depth, units = w_gate.shape[1], w_gate.shape[2]
+    width = depth // SUB
+    hc = heads // STEPS
+    f32, bf16, i32 = jnp.float32, jnp.bfloat16, jnp.int32
+    vmem = pl.BlockSpec(memory_space=pltpu.VMEM)
+    hbm = pl.BlockSpec(memory_space=pltpu.HBM)
+    dma = pltpu.SemaphoreType.DMA
+    scratch = [
+        pltpu.VMEM((SUB, width), f32),
+        pltpu.VMEM((4, 4, SUB, width), f32),
+        pltpu.VMEM((SUB, 16, width), bf16),
+        pltpu.VMEM((16, units), f32),
+        pltpu.VMEM((16, units), f32),
+        pltpu.VMEM((16, units), bf16),
+        pltpu.VMEM((4, 4, SUB, width), f32),
+        pltpu.VMEM((3, 4, SUB, width), f32),
+        pltpu.VMEM((4, SUB, width), f32),
+        pltpu.VMEM((4, SUB, width), f32),
+        pltpu.VMEM((heads, dim), f32),
+        pltpu.VMEM((depth, units), bf16),
+        pltpu.VMEM((depth, units), bf16),
+        pltpu.VMEM((units, depth), bf16),
+        pltpu.VMEM((STEPS, hc, dim, dim), bf16),
+        pltpu.VMEM(((STEPS + 1) // 2, hc, dim, dim), bf16),
+        pltpu.VMEM((STEPS, hc, dim, dim), bf16),
+        pltpu.VMEM((heads, dim, dim), bf16),
+        pltpu.VMEM((8, 128), f32),
+        pltpu.VMEM((3, 8, 128), f32),
+        pltpu.SMEM((1, parents.shape[0]), i32),
+        pltpu.SMEM(decay_rate.shape, f32),
+        pltpu.SMEM(expert_ids.shape, i32),
+        pltpu.SMEM(gate_weights.shape, f32),
+        pltpu.VMEM(qkv_rows.shape, bf16),
+        pltpu.VMEM(hidden.shape, bf16),
+        dma((6,)), dma((3,)), dma((3,)),
+        dma((3,)), dma((3,)), dma((3,)), dma((3,)), dma((3,)), dma((3,)), dma((3,)), dma((3,)),
+        dma((3, PIECES)), dma((STEPS,)), dma((STEPS,)),
+        dma((STEPS, 2)), dma((STEPS, 4)), dma((STEPS, 3)), dma((STEPS, 3)), dma((STEPS, 3)),
+    ]
+    scratch += [pltpu.VMEM((4, hc, dim, dim), bf16) for _ in range(STEPS)]
+    scratch += [pltpu.VMEM((SLOTS, hc, dim, dim), bf16) for _ in range(STEPS)]
+    new_states, readout, mixed, flag = pl.pallas_call(
+        routed_kernel,
+        out_shape=(
+            jax.ShapeDtypeStruct(states.shape, bf16),
+            jax.ShapeDtypeStruct(qkv_rows.shape[1:], bf16),
+            jax.ShapeDtypeStruct(hidden.shape, bf16),
+            jax.ShapeDtypeStruct((8, 128), f32),
+        ),
+        in_specs=[hbm] * 10,
+        out_specs=(hbm, vmem, vmem, vmem),
+        scratch_shapes=scratch,
+        compiler_params=pltpu.CompilerParams(
+            collective_id=1, has_side_effects=True, vmem_limit_bytes=50 * 1024 * 1024
+        ),
+        cost_estimate=pl.CostEstimate(
+            flops=6 * 16 * depth * units, bytes_accessed=6 * depth * units, transcendentals=0
+        ),
+    )(
+        parents.T, decay_rate, expert_ids, gate_weights, qkv_rows, hidden, states,
+        w_gate, w_up, w_down,
+    )
+
+    def again():
+        return fused(
+            states, qkv_rows, decay_rate, parents, hidden, expert_ids, gate_weights,
+            w_gate, w_up, w_down,
+        )
+
+    return lax.cond(flag[0, 0] > 0.5, again, lambda: (new_states, readout, mixed))
+
+
 def solution(mesh):
     in_specs = (
         P("expert", ("groups", "beam"), "head", None, None),
@@ -435,5 +949,5 @@
     )
     sizes = mesh.shape
     fits = sizes["expert"] == 8 and sizes["beam"] == 2 and sizes["head"] == 1
-    body = fused if fits else local
+    body = routed if fits else local
     return jax.shard_map(body, mesh=mesh, in_specs=in_specs, out_specs=out_specs, check_vma=False)

time: 71.3 us -> 59.8 us (0.84)
  Pallas kernels: 62.7 us -> 55.5 us
  local copies, waits for them, and re-layouts: 7.58 us -> 2.71 us
  between operations: 0.65 us -> 1.41 us
    pallas_call x1, Pallas kernels: 62.7 us -> 55.5 us  [routed(): pl.pallas_call(routed_kernel, out_shape=(jax.ShapeDtypeStruct(states.shap...]
    unnamed x16 -> x17, local copies, waits for them, and re-layouts: 7.58 us -> 2.2 us
where the time goes in v2:
time: 59.8 us; the launch traced here: 59.6 us
  Pallas kernels  55.5 us (93%)
  local copies, waits for them, and re-layouts  2.71 us (5%)
  between operations  1.41 us (2%)
    pallas_call x1, Pallas kernels, routed(): pl.pallas_call(routed_kernel, out_shape=(jax.ShapeDtypeStruct(states.shap...  55.5 us
    unnamed x17, local copies, waits for them, and re-layouts  2.2 us

profile of v2, /device:TPU:0, one launch (start us, length us, event | category | flops | bytes accessed | tf_op | source)
XLA Modules:
  0.0 59.6 jit_solution(2996745689095049200)
XLA Ops:
  0.6 0.0 copy-start
  0.6 0.0 copy-start.1
  0.7 0.0 copy-start.2
  0.7 0.0 copy-start.3
  0.7 0.0 copy-start.4
  0.7 0.0 copy-start.5
  0.7 0.0 copy-start.6
  0.7 55.5 %shard_map.127 = (bf16[1,1,32,128,128]{4,3,2,1,0:T(8,128)(2,1)S(1)}, bf16[1,1,32,128]{3,2,1,0:T(8,128)(2,1)S(1)}, bf16[1,1,3072]{2,1,0:T(2,128)(2,1)S(1)}, f32[8,128]{1,0:T(8,128)S(1)}) custom-call(s32[1,8]{1,0:T(1,128)} %bitcast.2, f32[1,1,32]{2,1,0:T(1,128)} %decay_in.1, s32[1,2,2]{2,1,0:T(2,128)} %ids_in.1, f32[1,2,2]{2,1,0:T(2,128)} %gates_in.1, ...), custom_call_target="tpu_custom_call" | custom-call | flops 339738624 | bytes 21233664 | tf_op jit(solution)/shard_map/pallas_call | solution.py:901
  56.2 0.5 slice.3
  57.4 0.0 copy-done
  57.4 0.0 copy-done.1
  57.4 0.0 copy-done.2
  57.4 0.0 copy-done.3
  57.4 0.0 copy-done.4
  57.4 0.0 copy-done.5
  57.4 0.0 copy-done.6
  57.5 1.0 %copy.29 = bf16[1,1,32,128,128]{4,3,2,1,0:T(8,128)(2,1)} copy(bf16[1,1,32,128,128]{4,3,2,1,0:T(8,128)(2,1)S(1)} %get-tuple-element.75) | data formatting | bytes 2097152
  58.4 0.6 %copy.30 = bf16[1,1,32,128]{3,2,1,0:T(8,128)(2,1)} copy(bf16[1,1,32,128]{3,2,1,0:T(8,128)(2,1)S(1)} %get-tuple-element.76) | data formatting | bytes 16384
  59.0 0.6 %copy.31 = bf16[1,1,3072]{2,1,0:T(2,128)(2,1)} copy(bf16[1,1,3072]{2,1,0:T(2,128)(2,1)S(1)} %get-tuple-element.77) | data formatting | bytes 12288
  (1 shorter events, 0.0 us)
Async XLA Ops:
  0.6 56.7 %copy-start = (bf16[1,1,32,128,128]{4,3,2,1,0:T(8,128)(2,1)S(1)}, bf16[1,1,32,128,128]{4,3,2,1,0:T(8,128)(2,1)}, u32[]{:S(2)}) copy-start(bf16[1,1,32,128,128]{4,3,2,1,0:T(8,128)(2,1)} %states.1) | copy-start | bytes 3145732
  0.6 56.7 %copy-start.1 = (bf16[3,1,1,32,128]{4,3,2,1,0:T(8,128)(2,1)S(1)}, bf16[3,1,1,32,128]{4,3,2,1,0:T(8,128)(2,1)}, u32[]{:S(2)}) copy-start(bf16[3,1,1,32,128]{4,3,2,1,0:T(8,128)(2,1)} %qkv_in.1) | copy-start | bytes 73732
  0.7 56.7 %copy-start.2 = (bf16[1,1,3072]{2,1,0:T(2,128)(2,1)S(1)}, bf16[1,1,3072]{2,1,0:T(2,128)(2,1)}, u32[]{:S(2)}) copy-start(bf16[1,1,3072]{2,1,0:T(2,128)(2,1)} %hid_in.1) | copy-start | bytes 18436
  0.7 56.7 %copy-start.3 = (s32[1,2,2]{2,1,0:T(2,128)S(1)}, s32[1,2,2]{2,1,0:T(2,128)}, u32[]{:S(2)}) copy-start(s32[1,2,2]{2,1,0:T(2,128)} %ids_in.1) | copy-start | bytes 52
  0.7 56.7 %copy-start.4 = (f32[1,2,2]{2,1,0:T(2,128)S(1)}, f32[1,2,2]{2,1,0:T(2,128)}, u32[]{:S(2)}) copy-start(f32[1,2,2]{2,1,0:T(2,128)} %gates_in.1) | copy-start | bytes 52
  0.7 56.7 %copy-start.5 = (f32[1,1,32]{2,1,0:T(1,128)S(1)}, f32[1,1,32]{2,1,0:T(1,128)}, u32[]{:S(2)}) copy-start(f32[1,1,32]{2,1,0:T(1,128)} %decay_in.1) | copy-start | bytes 388
  0.7 56.7 %copy-start.6 = (s32[8,1]{0,1:T(1,128)S(1)}, s32[8,1]{0,1:T(1,128)}, u32[]{:S(2)}) copy-start(s32[8,1]{0,1:T(1,128)} %param.15) | copy-start | bytes 100

commit v3 on v2

--- a/solution.py
+++ b/solution.py
@@ -417,6 +417,7 @@
 
 
 SLOTS = 3
+AHEAD = 4
 STEPS = 16
 
 
@@ -487,6 +488,16 @@
             states.at[0, 0, pl.ds(k * hc, hc)], near_set[k].at[c], own_sem.at[k]
         )
 
+    for k in range(steps):
+        own(k).start()
+    for p in range(PIECES):
+        span = pl.ds(p * (depth // PIECES), depth // PIECES)
+        pltpu.make_async_copy(w_gate.at[0, span], wg.at[span], w_sem.at[0, p]).start()
+        pltpu.make_async_copy(w_up.at[0, span], wu.at[span], w_sem.at[1, p]).start()
+    for p in range(PIECES):
+        span = pl.ds(p * (hidden_units // PIECES), hidden_units // PIECES)
+        pltpu.make_async_copy(w_down.at[0, span], wd.at[span], w_sem.at[2, p]).start()
+
     small[0].wait()
     for j in range(SUB):
         row[j : j + 1, :] = hid[0, :, j * width : (j + 1) * width].astype(f32)
@@ -590,16 +601,18 @@
             edged.at[k], far_set[k].at[0], pick_send.at[k, 2], b_recv.at[k, 0], edge, be
         )
 
-    for k in range(steps):
+    def send_own(k):
         @pl.when(outer)
         def _():
             state_copy(k, 1, near, 2 + c).start()
 
         state_copy(k, 0, sib, c).start()
-        own(k).start()
-        if k == 0:
-            for step in range(1, 4):
-                row_copy(step).start()
+
+    send_own(0)
+    for step in range(1, 4):
+        row_copy(step).start()
+    for k in range(1, AHEAD):
+        send_own(k)
 
     def mark_copy(step):
         column = (g * 2 + be + step) % 4
@@ -610,16 +623,9 @@
             device_id_type=pl.DeviceIdType.MESH,
         )
 
-    for step in range(1, 4):
-        mark_copy(step).start()
-
-    for p in range(PIECES):
-        span = pl.ds(p * (depth // PIECES), depth // PIECES)
-        pltpu.make_async_copy(w_gate.at[0, span], wg.at[span], w_sem.at[0, p]).start()
-        pltpu.make_async_copy(w_up.at[0, span], wu.at[span], w_sem.at[1, p]).start()
-    for p in range(PIECES):
-        span = pl.ds(p * (hidden_units // PIECES), hidden_units // PIECES)
-        pltpu.make_async_copy(w_down.at[0, span], wd.at[span], w_sem.at[2, p]).start()
+    def send_marks():
+        for step in range(1, 4):
+            mark_copy(step).start()
 
     def pass_near(k):
         @pl.when(inner)
@@ -785,7 +791,7 @@
     columns = padded.T
     values = qkv[2, 0, 0].astype(f32)
 
-    work = [gather_first, gather_second]
+    work = [gather_first, gather_second, send_marks]
     work += [functools.partial(first_dots, p) for p in range(PIECES)]
     work += [activate]
     work += [functools.partial(second_dots, p) for p in range(PIECES)]
@@ -799,6 +805,8 @@
             pass_near(i + 1)
         if 0 <= i - lag < steps:
             pass_far(i - lag)
+        if i + AHEAD < steps:
+            send_own(i + AHEAD)
         for unit in work[i * share : (i + 1) * share]:
             unit()
         if 0 <= i - last < steps:
@@ -851,6 +859,15 @@
         def _():
             extra_copy(k).wait_send()
             far_forward(k, 2, 2).wait_send()
+
+
+def hand_on(a_in, b_in, c_in, a_out, b_out, c_out, sem):
+    pairs = ((a_in, a_out), (b_in, b_out), (c_in, c_out))
+    copies = [pltpu.make_async_copy(src, dst, sem.at[i]) for i, (src, dst) in enumerate(pairs)]
+    for copy in copies:
+        copy.start()
+    for copy in copies:
+        copy.wait()
 
 
 def routed(
@@ -926,7 +943,16 @@
             w_gate, w_up, w_down,
         )
 
-    return lax.cond(flag[0, 0] > 0.5, again, lambda: (new_states, readout, mixed))
+    outs = lax.cond(flag[0, 0] > 0.5, again, lambda: (new_states, readout, mixed))
+    return tuple(
+        pl.pallas_call(
+            hand_on,
+            out_shape=tuple(jax.ShapeDtypeStruct(x.shape, x.dtype) for x in outs),
+            in_specs=[hbm] * 3,
+            out_specs=(hbm,) * 3,
+            scratch_shapes=[dma((3,))],
+        )(*outs)
+    )
 
 
 def solution(mesh):

time: 59.8 us -> 58.6 us (0.980)
  local copies, waits for them, and re-layouts: 2.71 us -> 0.54 us
  Pallas kernels: 55.5 us -> 56.5 us
    unnamed x17 -> x14, local copies, waits for them, and re-layouts: 2.2 us -> 0.03 us
    pallas_call x0 -> x1, Pallas kernels: none -> 1 us  [routed(): pl.pallas_call(hand_on, out_shape=tuple((jax.ShapeDtypeStruct(x.shape, x....]
where the time goes in v3:
time: 58.6 us; the launch traced here: 58.5 us
  Pallas kernels  56.5 us (96%)
  between operations  1.41 us (2%)
    pallas_call x1, Pallas kernels, routed(): pl.pallas_call(routed_kernel, out_shape=(jax.ShapeDtypeStruct(states.shap...  55.5 us

profile of v3, /device:TPU:0, one launch (start us, length us, event | category | flops | bytes accessed | tf_op | source)
XLA Modules:
  0.0 58.5 jit_solution(17375770672169509025)
XLA Ops:
  0.6 0.0 copy-start
  0.6 0.0 copy-start.1
  0.7 0.0 copy-start.2
  0.7 0.0 copy-start.3
  0.7 0.0 copy-start.4
  0.7 0.0 copy-start.5
  0.7 0.0 copy-start.6
  0.7 55.5 %shard_map.121 = (bf16[1,1,32,128,128]{4,3,2,1,0:T(8,128)(2,1)S(1)}, bf16[1,1,32,128]{3,2,1,0:T(8,128)(2,1)S(1)}, bf16[1,1,3072]{2,1,0:T(2,128)(2,1)S(1)}, f32[8,128]{1,0:T(8,128)S(1)}) custom-call(s32[1,8]{1,0:T(1,128)} %bitcast.2, f32[1,1,32]{2,1,0:T(1,128)} %decay_in.1, s32[1,2,2]{2,1,0:T(2,128)} %ids_in.1, f32[1,2,2]{2,1,0:T(2,128)} %gates_in.1, ...), custom_call_target="tpu_custom_call" | custom-call | flops 339738624 | bytes 21233664 | tf_op jit(solution)/shard_map/pallas_call | solution.py:918
  56.2 0.5 slice.3
  57.4 0.0 copy-done
  57.4 0.0 copy-done.1
  57.4 0.0 copy-done.2
  57.4 0.0 copy-done.3
  57.4 0.0 copy-done.4
  57.4 0.0 copy-done.5
  57.4 0.0 copy-done.6
  57.5 1.0 %shard_map.122 = (bf16[1,1,32,128,128]{4,3,2,1,0:T(8,128)(2,1)}, bf16[1,1,32,128]{3,2,1,0:T(8,128)(2,1)}, bf16[1,1,3072]{2,1,0:T(2,128)(2,1)}) custom-call(bf16[1,1,32,128,128]{4,3,2,1,0:T(8,128)(2,1)S(1)} %get-tuple-element.50.a_in, bf16[1,1,32,128]{3,2,1,0:T(8,128)(2,1)S(1)} %get-tuple-element.51.b_in, bf16[1,1,3072]{2,1,0:T(2,128)(2,1)S(1)} %get-tuple-element.52.c_in), custom_call_target="tpu_custom_call" | custom-call | tf_op jit(solution)/shard_map/pallas_call | solution.py:948
  (1 shorter events, 0.0 us)
Async XLA Ops:
  0.6 56.7 %copy-start = (bf16[1,1,32,128,128]{4,3,2,1,0:T(8,128)(2,1)S(1)}, bf16[1,1,32,128,128]{4,3,2,1,0:T(8,128)(2,1)}, u32[]{:S(2)}) copy-start(bf16[1,1,32,128,128]{4,3,2,1,0:T(8,128)(2,1)} %states.1) | copy-start | bytes 3145732
  0.6 56.7 %copy-start.1 = (bf16[3,1,1,32,128]{4,3,2,1,0:T(8,128)(2,1)S(1)}, bf16[3,1,1,32,128]{4,3,2,1,0:T(8,128)(2,1)}, u32[]{:S(2)}) copy-start(bf16[3,1,1,32,128]{4,3,2,1,0:T(8,128)(2,1)} %qkv_in.1) | copy-start | bytes 73732
  0.7 56.7 %copy-start.2 = (bf16[1,1,3072]{2,1,0:T(2,128)(2,1)S(1)}, bf16[1,1,3072]{2,1,0:T(2,128)(2,1)}, u32[]{:S(2)}) copy-start(bf16[1,1,3072]{2,1,0:T(2,128)(2,1)} %hid_in.1) | copy-start | bytes 18436
  0.7 56.7 %copy-start.3 = (s32[1,2,2]{2,1,0:T(2,128)S(1)}, s32[1,2,2]{2,1,0:T(2,128)}, u32[]{:S(2)}) copy-start(s32[1,2,2]{2,1,0:T(2,128)} %ids_in.1) | copy-start | bytes 52
  0.7 56.7 %copy-start.4 = (f32[1,2,2]{2,1,0:T(2,128)S(1)}, f32[1,2,2]{2,1,0:T(2,128)}, u32[]{:S(2)}) copy-start(f32[1,2,2]{2,1,0:T(2,128)} %gates_in.1) | copy-start | bytes 52
  0.7 56.7 %copy-start.5 = (f32[1,1,32]{2,1,0:T(1,128)S(1)}, f32[1,1,32]{2,1,0:T(1,128)}, u32[]{:S(2)}) copy-start(f32[1,1,32]{2,1,0:T(1,128)} %decay_in.1) | copy-start | bytes 388
  0.7 56.7 %copy-start.6 = (s32[8,1]{0,1:T(1,128)S(1)}, s32[8,1]{0,1:T(1,128)}, u32[]{:S(2)}) copy-start(s32[8,1]{0,1:T(1,128)} %param.15) | copy-start | bytes 100
